TPU v7x, 32 devices: a whole 2x2x4 slice. The times are simulated.
32 devices in a mesh: groups: 2 (over y), owners: 4 (over z), feat: 2 (over x), rep: 2 (over core).
Axes of the slice: x: 2, y: 2, z: 4, core: 2. Of those that a mesh axis runs over, the one named last changes fastest.
Arguments:
- emb: bfloat16 [16384, 4096], P(('groups', 'owners', 'rep'), 'feat'), parts along dimension 0, as said below
- basis: bfloat16 [4096, 256], P('feat'), may hold values from -0.09375 to 0.09375
- labels: int32 [16384], P(('groups', 'owners', 'rep', 'feat')), parts along dimension 0, may hold values from 0 to 63, as said below
- owner_map: int32 [128], P('groups'), parts along dimension 0, may hold values from 0 to 63, as said below
- order: int32 [16384], P(('groups', 'owners', 'rep', 'feat')), parts along dimension 0, may hold values from 0 to 8191, each once
Outputs:
- best: float32 [16384], P(('groups', 'owners', 'rep', 'feat')), parts along dimension 0
There are 2 independent parts, one for each index of `groups`. A program takes and returns all parts, laid end to end along the dimension named above; an argument that names none is the same for every part. Nothing has to cross between parts.
Inputs may be any that keep to these rules, and one draw needn't show every extreme that they name: `labels`: among the rows of one device at most 128 have slots in one owner column (slot // 8); some owner column receives exactly 128 from every device. `owner_map`: A permutation of the clusters. `emb`: rows cluster around a center of their cluster.
All inputs are finite; a program needn't handle non-finite values.
Results may differ from a plain program's by a relative error of at most 0.0055.
Values may be sent and summed in bfloat16 or wider, within the bound.
A program may use at most 64 MiB of HBM per device.

v0:
```python
import jax
import jax.numpy as jnp
from jax import lax
from jax.sharding import PartitionSpec as P


def unitize(diff):
    scale = lax.rsqrt(jnp.mean(diff * diff, axis=-1, keepdims=True) + 1e-06)
    return (diff * scale / jnp.sqrt(jnp.float32(diff.shape[-1]))).astype(jnp.bfloat16)


def per_device(emb, basis, labels, owner_map, order):
    row_dev = labels.shape[0]
    width = basis.shape[1]
    n_own = lax.axis_size("owners")
    n_col = lax.axis_size("feat")
    n_dest = n_own * n_col
    nclust = owner_map.shape[0]
    cl_dest = nclust // n_dest
    cap = 2 * row_dev // n_dest
    proj = lax.psum_scatter(
        jnp.dot(emb, basis, preferred_element_type=jnp.float32),
        "feat",
        scatter_dimension=0,
        tiled=True,
    ).astype(jnp.bfloat16)
    cluster_ids = jnp.arange(nclust, dtype=jnp.int32)
    slot = jnp.sum(
        jnp.where(labels[:, None] == cluster_ids[None, :], owner_map[None, :], 0), axis=1
    )
    dest = slot // cl_dest
    dest_hot = (dest[:, None] == jnp.arange(n_dest, dtype=jnp.int32)[None, :]).astype(jnp.int32)
    rank = jnp.sum(jnp.cumsum(dest_hot, axis=0) * dest_hot, axis=1) - 1
    place = dest * cap + rank
    member = (slot[:, None] == cluster_ids[None, :]).astype(jnp.bfloat16)
    sums = lax.dot_general(
        member, proj, (((0,), (0,)), ((), ())), preferred_element_type=jnp.float32
    )
    counts = jnp.sum(member.astype(jnp.float32), axis=0)
    all_sums, all_counts = lax.psum((sums, counts), ("owners", "feat", "rep"))
    centre = jnp.take(all_sums, slot, axis=0) / jnp.take(all_counts, slot)[:, None]
    payload = unitize(proj.astype(jnp.float32) - centre)
    vec_buf = jnp.zeros((n_dest * cap, width), jnp.bfloat16).at[place].set(payload)
    slot_buf = jnp.full((n_dest * cap,), -1, jnp.int32).at[place].set(slot)
    order_buf = jnp.zeros((n_dest * cap,), jnp.int32).at[place].set(order)
    got_vec, got_slot, got_order = (
        lax.all_to_all(
            vec_buf.reshape(n_dest, cap, width),
            ("owners", "feat"),
            split_axis=0,
            concat_axis=0,
            tiled=True,
        ),
        lax.all_to_all(
            slot_buf.reshape(n_dest, cap),
            ("owners", "feat"),
            split_axis=0,
            concat_axis=0,
            tiled=True,
        ),
        lax.all_to_all(
            order_buf.reshape(n_dest, cap),
            ("owners", "feat"),
            split_axis=0,
            concat_axis=0,
            tiled=True,
        ),
    )
    held = n_dest * cap
    got_vec = got_vec.reshape(held, width)
    got_slot = got_slot.reshape(held)
    got_order = got_order.reshape(held)
    start_best = jnp.full((held,), -1.0, jnp.float32)
    keys = lax.all_gather(got_vec, "rep", axis=0, tiled=True)
    key_slot = lax.all_gather(got_slot, "rep", axis=0, tiled=True)
    key_order = lax.all_gather(got_order, "rep", axis=0, tiled=True)
    scores = lax.dot_general(
        got_vec, keys, (((1,), (1,)), ((), ())), preferred_element_type=jnp.float32
    )
    mask = (
        (got_slot[:, None] == key_slot[None, :])
        & (key_order[None, :] < got_order[:, None])
        & (key_slot[None, :] >= 0)
    )
    found = jnp.maximum(start_best, jnp.max(jnp.where(mask, scores, jnp.float32(-1.0)), axis=1))
    back = lax.all_to_all(
        found.reshape(n_dest, cap), ("owners", "feat"), split_axis=0, concat_axis=0, tiled=True
    )
    return jnp.take(back.reshape(held), place)


def solution(mesh):
    return jax.shard_map(
        per_device,
        mesh=mesh,
        in_specs=(
            P(("groups", "owners", "rep"), "feat"),
            P("feat", None),
            P(("groups", "owners", "rep", "feat")),
            P("groups"),
            P(("groups", "owners", "rep", "feat")),
        ),
        out_specs=P(("groups", "owners", "rep", "feat")),
        check_vma=False,
    )
```

profile of v0, /device:TPU:0, one launch (start us, length us, event | category | flops | bytes accessed | tf_op | source)
XLA Modules:
  0.0 248.2 jit_solution(5327198917547531272)
XLA Ops:
  6.5 1.2 copy-done
  7.8 4.4 %fusion.23 = f32[1024,256]{1,0:T(8,128)} fusion(bf16[1024,2048]{1,0:T(8,128)(2,1)} %param.5, bf16[2048,256]{1,0:T(8,128)(2,1)S(1)} %copy-done), kind=kOutput, calls=%fused_computation.68 | convolution fusion | flops 1073741824 | bytes 6291456 | tf_op jit(solution)/shard_map/dot_general | solution.py:22
  12.3 0.1 select_reduce_fusion.1
  12.4 1.1 reduce-window.6
  13.6 0.2 slice_reduce_fusion
  13.8 0.1 convert_reduce_fusion
  13.9 35.2 %psum.15 = f32[64]{0:T(128)S(1)} all-reduce(f32[64]{0:T(128)S(1)} %convert_reduce_fusion), channel_id=1, replica_groups=mesh['groups'=2,'owners'=4,'feat'=2,'rep'=2] {'owners','feat','rep'}, use_global_device_ids=true, to_apply=%region_9.10 | all-reduce | flops 64 | bytes 512 | tf_op jit(solution)/shard_map/psum | solution.py:40
  49.1 0.7 fusion.22
  49.8 0.7 fusion.19
  50.5 0.7 fusion.20
  51.3 0.7 fusion.21
  52.1 39.9 %select_select_fusion = (f32[512]{0:T(512)S(1)}, pred[512]{0:T(512)(128)(4,1)S(1)}) fusion(s32[512]{0:T(512)S(1)} %bitcast.107, f32[]{:T(128)} %bitcast.11, f32[]{:T(128)} %bitcast.12, f32[]{:T(128)} %bitcast.13, f32[]{:T(128)} %bitcast.14, f32[]{:T(128)} %bitcast.15, f32[]{:T(128)} %bitcast.16, f32[]{:T(128)} %bitcast.17, f32[]{:T(128)} %bitcast.18, ...), kind=kLoop, calls=%fused_computation.51 | loop fusion | flops 68096 | bytes 6912 | tf_op jit(solution)/shard_map/jit(_take)/select_n | solution.py:41
  92.1 1.9 fusion.5
  94.1 81.8 %all-reduce.2.cloned.1.call-done = f32[64,256]{1,0:T(8,128)} async-done(((f32[64,256]{1,0:T(8,128)}), f32[64,256]{1,0:T(8,128)}) %all-reduce.2.cloned.1.call-update) | async-done | bytes 65552 | tf_op jit(solution)/shard_map/psum | solution.py:40
  175.9 2.4 gather_fusion
  178.3 0.3 multiply_reduce_fusion
  178.6 2.6 %scatter_custom_fusion.2 = bf16[1024,256]{1,0:T(8,128)(2,1)S(1)} fusion(s32[512]{0:T(512)S(1)} %bitcast.113, f32[512,256]{1,0:T(8,128)S(1)} %get-tuple-element.6, f32[]{:T(128)} %constant.85.clone.1, f32[512]{0:T(512)S(1)} %add_rsqrt_fusion, bf16[]{:T(256)} %constant.78.clone.1), kind=kCustom, calls=%fused_computation.9 | custom fusion | flops 393216 | bytes 1050630 | tf_op jit(solution)/shard_map/scatter | solution.py:43
  181.2 18.5 %all_to_all.29 = bf16[8,128,256]{2,1,0:T(8,128)(2,1)} all-to-all(bf16[8,128,256]{2,1,0:T(8,128)(2,1)S(1)} %bitcast.103), channel_id=1, replica_groups=mesh['groups'=2,'owners'=4,'feat'=2,'rep'=2] {'owners','feat'}, dimensions={0} | all-to-all | bytes 1048576 | tf_op jit(solution)/shard_map/all_to_all | solution.py:47
  199.7 3.2 %scatter_custom_fusion.1 = s32[1024]{0:T(1024)} fusion(s32[512]{0:T(512)S(1)} %bitcast.114, s32[512]{0:T(512)} %param.9, s32[]{:T(128)} %constant.47.clone.1), kind=kCustom, calls=%fused_computation.54 | custom fusion | bytes 4608 | tf_op jit(solution)/shard_map/scatter | solution.py:45
  202.9 3.6 %all-to-all-start.1 = ((s32[8,1,128]{2,1,0:T(1,128)}), s32[8,1,128]{2,1,0:T(1,128)S(1)}, u32[]{:S(2)}, u32[]{:S(2)}) async-start(s32[8,1,128]{2,1,0:T(1,128)} %bitcast.8), calls=%async_computation.1 | async-start | bytes 8192 | tf_op jit(solution)/shard_map/all_to_all | solution.py:61
  206.5 3.0 %scatter_custom_fusion = s32[1024]{0:T(1024)} fusion(s32[512]{0:T(512)S(1)} %bitcast.115, s32[512]{0:T(512)S(1)} %select_reduce_fusion.1, s32[]{:T(128)} %constant.51.clone.1), kind=kCustom, calls=%fused_computation.56 | custom fusion | bytes 4100 | tf_op jit(solution)/shard_map/scatter | solution.py:44
  209.6 3.5 %all-to-all-done.1 = s32[8,1,128]{2,1,0:T(1,128)S(1)} async-done(((s32[8,1,128]{2,1,0:T(1,128)}), s32[8,1,128]{2,1,0:T(1,128)S(1)}, u32[]{:S(2)}, u32[]{:S(2)}) %all-to-all-start.1) | async-done | bytes 4128 | tf_op jit(solution)/shard_map/all_to_all | solution.py:61
  213.0 3.3 %all-to-all-start = ((s32[8,1,128]{2,1,0:T(1,128)}), s32[8,1,128]{2,1,0:T(1,128)S(1)}, u32[]{:S(2)}, u32[]{:S(2)}) async-start(s32[8,1,128]{2,1,0:T(1,128)} %bitcast.6), calls=%async_computation | async-start | bytes 8192 | tf_op jit(solution)/shard_map/all_to_all | solution.py:54
  216.3 1.8 all_gather.10
  218.1 4.6 %all-to-all-done = s32[8,1,128]{2,1,0:T(1,128)S(1)} async-done(((s32[8,1,128]{2,1,0:T(1,128)}), s32[8,1,128]{2,1,0:T(1,128)S(1)}, u32[]{:S(2)}, u32[]{:S(2)}) %all-to-all-start) | async-done | bytes 4128 | tf_op jit(solution)/shard_map/all_to_all | solution.py:54
  222.7 1.8 all_gather.9
  224.5 3.9 %select_reduce_fusion = f32[1024]{0:T(1024)S(1)} fusion(bf16[1024,256]{1,0:T(8,128)(2,1)} %bitcast.105, bf16[2048,256]{1,0:T(8,128)(2,1)} %all-gather.2.cloned.1.call-done, s32[2048]{0:T(1024)S(1)} %all_gather.10, s32[2048]{0:T(1024)S(1)} %all_gather.9, s32[1024]{0:T(1024)S(1)} %bitcast.110, s32[1024]{0:T(1024)S(1)} %bitcast.112, ...), kind=kOutput, calls=%fused_computation.5 | convolution fusion | flops 1086323712 | bytes 1603584 | tf_op jit(solution)/shard_map/dot_general | solution.py:77
  228.5 0.6 broadcast_maximum_fusion
  229.1 3.3 %all-to-all-start.3 = ((f32[8,1,128]{2,1,0:T(1,128)}), f32[8,1,128]{2,1,0:T(1,128)S(1)}, u32[]{:S(2)}, u32[]{:S(2)}) async-start(f32[8,1,128]{2,1,0:T(1,128)} %bitcast.77), calls=%async_computation.4 | async-start | bytes 8192 | tf_op jit(solution)/shard_map/all_to_all | solution.py:86
  232.4 6.4 %all-to-all-done.3 = f32[8,1,128]{2,1,0:T(1,128)S(1)} async-done(((f32[8,1,128]{2,1,0:T(1,128)}), f32[8,1,128]{2,1,0:T(1,128)S(1)}, u32[]{:S(2)}, u32[]{:S(2)}) %all-to-all-start.3) | async-done | bytes 4128 | tf_op jit(solution)/shard_map/all_to_all | solution.py:86
  238.8 2.3 gather_fusion.1
  241.1 0.6 and_select_fusion.1
  (27 shorter events, 0.4 us)
Async XLA Ops:
  6.5 1.2 copy-start
  6.5 5.7 %copy-start.3 = (s32[64]{0:T(128)S(1)}, s32[64]{0:T(128)}, u32[]{:S(2)}) copy-start(s32[64]{0:T(128)} %param.8) | copy-start | bytes 772
  6.5 5.7 %copy-start.2 = (s32[512]{0:T(512)S(1)}, s32[512]{0:T(512)}, u32[]{:S(2)}) copy-start(s32[512]{0:T(512)} %param.7) | copy-start | bytes 6148
  6.5 85.5 %reduce-scatter.2.cloned.1.call-start = ((), (), s32[]{:S(2)}) async-start(), calls=%async_computation.5 | async-start | bytes 1572864 | tf_op jit(solution)/shard_map/reduce_scatter | solution.py:21
  12.2 163.6 %all-reduce.2.cloned.1.call-start = ((), (), s32[]{:S(2)}) async-start(), calls=%async_computation.6 | async-start | bytes 131072 | tf_op jit(solution)/shard_map/psum | solution.py:40
  92.1 86.2 %copy-start.1 = (f32[512,256]{1,0:T(8,128)S(1)}, f32[512,256]{1,0:T(8,128)}, u32[]{:S(2)}) copy-start(f32[512,256]{1,0:T(8,128)} %reduce-scatter.2.cloned.1.call-done) | copy-start | bytes 1572868
  94.0 130.5 %all-gather.2.cloned.1.call-start = ((), (), s32[]{:S(2)}) async-start(), calls=%async_computation.7 | async-start | bytes 1572864 | tf_op jit(solution)/shard_map/all_gather | solution.py:74
  202.9 10.1 %all-to-all-start.1 = ((s32[8,1,128]{2,1,0:T(1,128)}), s32[8,1,128]{2,1,0:T(1,128)S(1)}, u32[]{:S(2)}, u32[]{:S(2)}) async-start(s32[8,1,128]{2,1,0:T(1,128)} %bitcast.8), calls=%async_computation.1 | async-start | bytes 8192 | tf_op jit(solution)/shard_map/all_to_all | solution.py:61
  213.0 9.7 %all-to-all-start = ((s32[8,1,128]{2,1,0:T(1,128)}), s32[8,1,128]{2,1,0:T(1,128)S(1)}, u32[]{:S(2)}, u32[]{:S(2)}) async-start(s32[8,1,128]{2,1,0:T(1,128)} %bitcast.6), calls=%async_computation | async-start | bytes 8192 | tf_op jit(solution)/shard_map/all_to_all | solution.py:54
  229.1 9.7 %all-to-all-start.3 = ((f32[8,1,128]{2,1,0:T(1,128)}), f32[8,1,128]{2,1,0:T(1,128)S(1)}, u32[]{:S(2)}, u32[]{:S(2)}) async-start(f32[8,1,128]{2,1,0:T(1,128)} %bitcast.77), calls=%async_computation.4 | async-start | bytes 8192 | tf_op jit(solution)/shard_map/all_to_all | solution.py:86
Sparse Core Ops, SparseCore 0:
  12.3 23.2 reduce-scatter.1
  94.1 81.6 all-reduce.1
  199.9 8.0 all-gather.1
where the time goes:
time: 249 us; the launch traced here: 248 us
  waiting for transfers between devices  96.3 us (39%)
  blocking collectives  57.3 us (23%)
  other arithmetic  45.6 us (18%)
  local copies, waits for them, and re-layouts  15.2 us (6%)
  between operations  13.3 us (5%)
  starting transfers between devices  10.4 us (4%)
  matrix products  10.3 us (4%)
    psum x1, waiting for transfers between devices, per_device(): all_sums, all_counts = lax.psum((sums, counts), ('owners', 'feat', 'rep'))  81.8 us
    select_n x1, other arithmetic, per_device(): jnp.take(all_counts, slot)[:, None]  39.9 us
    psum x1, blocking collectives, per_device(): all_sums, all_counts = lax.psum((sums, counts), ('owners', 'feat', 'rep'))  35.2 us
    all_to_all x1, blocking collectives, per_device(): lax.all_to_all(vec_buf.reshape(n_dest, cap, width), ('owners', 'feat'), s...  18.5 us
    all_to_all x1, waiting for transfers between devices, per_device(): lax.all_to_all(found.reshape(n_dest, cap), ('owners', 'feat'), split_axis...  6.39 us
  transfers between devices with their start and end apart: 6, of which 4 were waited for; matrix products, arithmetic and copies ran while one was open for 20% of the time, Pallas kernels for 0%

commit v1 on v0

--- a/solution.py
+++ b/solution.py
@@ -1,6 +1,10 @@
+import functools
+
 import jax
 import jax.numpy as jnp
 from jax import lax
+from jax.experimental import pallas as pl
+from jax.experimental.pallas import tpu as pltpu
 from jax.sharding import PartitionSpec as P
 
 
@@ -9,7 +13,7 @@
     return (diff * scale / jnp.sqrt(jnp.float32(diff.shape[-1]))).astype(jnp.bfloat16)
 
 
-def per_device(emb, basis, labels, owner_map, order):
+def per_device_plain(emb, basis, labels, owner_map, order):
     row_dev = labels.shape[0]
     width = basis.shape[1]
     n_own = lax.axis_size("owners")
@@ -89,6 +93,283 @@
     return jnp.take(back.reshape(held), place)
 
 
+LANES = 128
+CHUNKS = 4
+
+
+def split3(v):
+    hi = v.astype(jnp.bfloat16).astype(jnp.float32)
+    mid = (v - hi).astype(jnp.bfloat16).astype(jnp.float32)
+    return hi, mid, v - hi - mid
+
+
+def window_kernel(
+    n_dest, n_feat, cap,
+    emb, basis, labels, owner_map, order, out,
+    emb_v, basis_v, own, part_send, part_recv, place_hot, buf, meta_send, meta, rows, unit,
+    score_send, back,
+    load_sem, part_ssem, part_rsem, meta_ssem, meta_rsem, vec_ssem, vec_rsem,
+    fwd_ssem, fwd_rsem, back_ssem, back_rsem,
+):
+    f32, bf16 = jnp.float32, jnp.bfloat16
+    half = part_send.shape[0]
+    width = part_send.shape[1]
+    held = n_dest * cap
+    step = half // CHUNKS
+    n_col = width // LANES
+    nclust = owner_map.shape[1]
+    cl_dest = nclust // n_dest
+    feat = lax.axis_index("feat")
+    rep = lax.axis_index("rep")
+    me = lax.axis_index("owners") * n_feat + feat
+    other = 1 - rep
+
+    def device(column, r):
+        return {"owners": column // n_feat, "feat": column % n_feat, "rep": r}
+
+    def column_at(k):
+        return lax.rem(me + k, n_dest)
+
+    def block(column):
+        return pl.ds(pl.multiple_of(column * cap, cap), cap)
+
+    def remote(src, dst, ssem, rsem, to):
+        return pltpu.make_async_remote_copy(
+            src_ref=src, dst_ref=dst, send_sem=ssem, recv_sem=rsem,
+            device_id=to, device_id_type=pl.DeviceIdType.MESH,
+        )
+
+    barrier = pltpu.get_barrier_semaphore()
+    for k in range(n_dest):
+        if k:
+            pl.semaphore_signal(barrier, inc=1, device_id=device(column_at(k), rep),
+                                device_id_type=pl.DeviceIdType.MESH)
+        pl.semaphore_signal(barrier, inc=1, device_id=device(column_at(k), other),
+                            device_id_type=pl.DeviceIdType.MESH)
+
+    loads = [pltpu.make_async_copy(basis, basis_v, load_sem.at[2 * CHUNKS])]
+    for c in range(2 * CHUNKS):
+        side = 1 - feat if c < CHUNKS else feat
+        at = pl.multiple_of(side * half + (c % CHUNKS) * step, step)
+        loads.append(pltpu.make_async_copy(
+            emb.at[pl.ds(at, step), :], emb_v.at[pl.ds(c * step, step), :], load_sem.at[c]))
+    for load in loads:
+        load.start()
+
+    omap = owner_map[...].astype(f32)
+    eye = (lax.broadcasted_iota(jnp.int32, (nclust, nclust), 0)
+           == lax.broadcasted_iota(jnp.int32, (nclust, nclust), 1))
+    omap_col = jnp.sum(jnp.where(eye, omap, 0.0), axis=1, keepdims=True)
+    label_hot = lax.broadcasted_iota(jnp.int32, (nclust, half), 0) == labels[...]
+    slot = jnp.sum(jnp.where(label_hot, omap_col, 0.0), axis=0, keepdims=True)
+    dest = jnp.floor(slot * (1.0 / cl_dest))
+    local = slot - dest * cl_dest
+    dest_hot = lax.broadcasted_iota(jnp.int32, (n_dest, half), 0) == dest.astype(jnp.int32)
+    upto = (lax.broadcasted_iota(jnp.int32, (half, half), 0)
+            <= lax.broadcasted_iota(jnp.int32, (half, half), 1))
+    running = jnp.dot(
+        jnp.where(dest_hot, 1.0, 0.0).astype(bf16), jnp.where(upto, 1.0, 0.0).astype(bf16),
+        preferred_element_type=f32)
+    rank = jnp.sum(jnp.where(dest_hot, running, 0.0), axis=0, keepdims=True) - 1.0
+    place = (dest * cap + rank).astype(jnp.int32)
+
+    peer = {"feat": 1 - feat}
+    part_copies = [[], []]
+    loads[0].wait()
+    for c in range(CHUNKS):
+        at = pl.ds(c * step, step)
+        loads[1 + c].wait()
+        part_send[at, :] = jnp.dot(
+            emb_v[at, :], basis_v[...], preferred_element_type=f32).astype(bf16)
+        if c == 0:
+            pl.semaphore_wait(barrier, 2 * n_dest - 1)
+        cut = (at, pl.ds(0, LANES))
+        copy = remote(part_send.at[cut], part_recv.at[cut], part_ssem.at[c], part_rsem.at[c], peer)
+        copy.start()
+        part_copies[0].append(copy)
+    for n in range(1, n_col):
+        cut = (slice(None), pl.ds(n * LANES, LANES))
+        copy = remote(part_send.at[cut], part_recv.at[cut], part_ssem.at[CHUNKS + n - 1],
+                      part_rsem.at[CHUNKS + n - 1], peer)
+        copy.start()
+        part_copies[n].append(copy)
+
+    place_hot[...] = jnp.where(
+        lax.broadcasted_iota(jnp.int32, (held, half), 0) == place, 1.0, 0.0).astype(bf16)
+    ranks = order[...]
+    pieces = jnp.concatenate([
+        local + 1.0,
+        lax.shift_right_logical(ranks, 14).astype(f32),
+        (lax.shift_right_logical(ranks, 7) & 127).astype(f32),
+        (ranks & 127).astype(f32),
+        jnp.zeros((4, half), f32)], axis=0).astype(bf16)
+    placed = lax.dot_general(pieces, place_hot[...], (((1,), (1,)), ((), ())),
+                             preferred_element_type=f32)
+    meta_send[...] = jnp.zeros_like(meta_send)
+    meta_send[0:1, :] = placed[0:1, :]
+    meta_send[1:2, :] = placed[1:2, :] * 16384.0 + placed[2:3, :] * 128.0 + placed[3:4, :]
+    meta_copies = []
+    for k in range(n_dest):
+        to = column_at(k)
+        if k:
+            meta_copies.append(remote(
+                meta_send.at[:, block(to)], meta.at[0, :, block(me)],
+                meta_ssem.at[k], meta_rsem.at[k], device(to, rep)))
+        meta_copies.append(remote(
+            meta_send.at[:, block(to)], meta.at[1, :, block(me)],
+            meta_ssem.at[n_dest + k], meta_rsem.at[n_dest + k], device(to, other)))
+    for copy in meta_copies:
+        copy.start()
+    meta[0, :, block(me)] = meta_send[:, block(me)]
+
+    for c in range(CHUNKS):
+        at = pl.ds(c * step, step)
+        loads[1 + CHUNKS + c].wait()
+        own[at, :] = jnp.dot(
+            emb_v[pl.ds((CHUNKS + c) * step, step), :], basis_v[...], preferred_element_type=f32)
+
+    vec_copies = [[None] * n_dest for _ in range(n_col)]
+    for n in range(n_col):
+        lanes = pl.ds(n * LANES, LANES)
+        for copy in part_copies[n]:
+            copy.wait_recv()
+        proj = (own[:, lanes] + part_recv[:, lanes].astype(f32)).astype(bf16)
+        buf[:, lanes] = jnp.dot(place_hot[...], proj, preferred_element_type=f32).astype(bf16)
+        for k in range(1, n_dest):
+            to = column_at(k)
+            copy = remote(buf.at[block(to), lanes], rows.at[0, block(me), lanes],
+                          vec_ssem.at[n, k], vec_rsem.at[n, k], device(to, rep))
+            copy.start()
+            vec_copies[n][k] = copy
+        rows[0, block(me), lanes] = buf[block(me), lanes]
+    for copies in part_copies:
+        for copy in copies:
+            copy.wait_send()
+
+    for copy in meta_copies:
+        copy.wait()
+    member = lax.broadcasted_iota(jnp.int32, (8, held), 0).astype(f32) + 1.0
+    hot = [jnp.where(meta[r, 0:1, :] == member, 1.0, 0.0) for r in range(2)]
+    counts = jnp.sum(hot[0], axis=1, keepdims=True) + jnp.sum(hot[1], axis=1, keepdims=True)
+    hot = [h.astype(bf16) for h in hot]
+
+    fwd_copies = []
+    for n in range(n_col):
+        lanes = pl.ds(n * LANES, LANES)
+        for k in range(n_dest):
+            came = lax.rem(me + n_dest - k, n_dest)
+            if k:
+                vec_copies[n][k].wait_recv()
+            copy = remote(rows.at[0, block(came), lanes], rows.at[1, block(came), lanes],
+                          fwd_ssem.at[n, k], fwd_rsem.at[n, k], {"rep": other})
+            copy.start()
+            fwd_copies.append(copy)
+    sums = jnp.dot(hot[0], rows[0], preferred_element_type=f32)
+    for copies in vec_copies:
+        for copy in copies[1:]:
+            copy.wait_send()
+    cols = [jnp.transpose(meta[r]) for r in range(2)]
+    for copy in fwd_copies:
+        copy.wait()
+    sums = sums + jnp.dot(hot[1], rows[1], preferred_element_type=f32)
+
+    centre = jnp.where(counts > 0.0, sums / jnp.maximum(counts, 1.0), 0.0)
+    centre3 = jnp.concatenate(
+        list(split3(centre)) + [jnp.zeros((LANES - 24, width), f32)], axis=0).astype(bf16)
+    lane = lax.broadcasted_iota(jnp.int32, (held, LANES), 1)
+    want = jnp.where(lane < 24, (lane & 7) + 1, -1).astype(f32)
+    for r in range(2):
+        hot_col = jnp.where(cols[r][:, 0:1] == want, 1.0, 0.0).astype(bf16)
+        diff = rows[r].astype(f32) - jnp.dot(hot_col, centre3, preferred_element_type=f32)
+        mean = jnp.sum(diff * diff, axis=-1, keepdims=True) * (1.0 / width)
+        scale = lax.rsqrt(mean + 1e-06)
+        unit[r, :, :] = (diff * scale / jnp.sqrt(f32(width))).astype(bf16)
+
+    my_slot, my_order = meta[0, 0:1, :], meta[0, 1:2, :]
+    best = jnp.full((1, held), -1.0, f32)
+    tile = 256 if held % 256 == 0 else cap
+    for r in range(2):
+        from_slot = jnp.where(cols[r][:, 0:1] > 0.0, cols[r][:, 0:1], -5.0)
+        from_order = cols[r][:, 1:2]
+        for t in range(held // tile):
+            cut = slice(t * tile, (t + 1) * tile)
+            scores = lax.dot_general(unit[r, cut, :], unit[0], (((1,), (1,)), ((), ())),
+                                     preferred_element_type=f32)
+            mask = (from_slot[cut] == my_slot) & (from_order[cut] < my_order)
+            best = jnp.maximum(best, jnp.max(jnp.where(mask, scores, -1.0), axis=0, keepdims=True))
+
+    score_send[...] = jnp.concatenate(list(split3(best)) + [jnp.zeros((5, held), f32)], axis=0)
+    back_copies = []
+    for k in range(1, n_dest):
+        to = column_at(k)
+        copy = remote(score_send.at[:, block(to)], back.at[:, block(me)],
+                      back_ssem.at[k], back_rsem.at[k], device(to, rep))
+        copy.start()
+        back_copies.append(copy)
+    back[:, block(me)] = score_send[:, block(me)]
+    for copy in back_copies:
+        copy.wait()
+    mine = jnp.dot(back[...].astype(bf16), place_hot[...], preferred_element_type=f32)
+    out[...] = mine[0:1, :] + mine[1:2, :] + mine[2:3, :]
+
+
+def per_device(emb, basis, labels, owner_map, order):
+    n_feat = lax.axis_size("feat")
+    n_dest = lax.axis_size("owners") * n_feat
+    row_dev = labels.shape[0]
+    depth, width = basis.shape
+    cap = 2 * row_dev // n_dest
+    nclust = owner_map.shape[0]
+    fits = (
+        n_feat == 2 and lax.axis_size("rep") == 2 and cap % LANES == 0 and width == 2 * LANES
+        and row_dev % (16 * CHUNKS) == 0 and nclust == 8 * n_dest and n_dest <= 8
+    )
+    if not fits:
+        return per_device_plain(emb, basis, labels, owner_map, order)
+    held = n_dest * cap
+    n_col = width // LANES
+    dma = pltpu.SemaphoreType.DMA
+    vmem = pl.BlockSpec(memory_space=pltpu.VMEM)
+    hbm = pl.BlockSpec(memory_space=pl.ANY)
+    best = pl.pallas_call(
+        functools.partial(window_kernel, n_dest, n_feat, cap),
+        out_shape=jax.ShapeDtypeStruct((1, row_dev), jnp.float32),
+        in_specs=[hbm, hbm, vmem, vmem, vmem],
+        out_specs=vmem,
+        scratch_shapes=[
+            pltpu.VMEM((n_feat * row_dev, depth), jnp.bfloat16),
+            pltpu.VMEM((depth, width), jnp.bfloat16),
+            pltpu.VMEM((row_dev, width), jnp.float32),
+            pltpu.VMEM((row_dev, width), jnp.bfloat16),
+            pltpu.VMEM((row_dev, width), jnp.bfloat16),
+            pltpu.VMEM((held, row_dev), jnp.bfloat16),
+            pltpu.VMEM((held, width), jnp.bfloat16),
+            pltpu.VMEM((8, held), jnp.float32),
+            pltpu.VMEM((2, 8, held), jnp.float32),
+            pltpu.VMEM((2, held, width), jnp.bfloat16),
+            pltpu.VMEM((2, held, width), jnp.bfloat16),
+            pltpu.VMEM((8, held), jnp.float32),
+            pltpu.VMEM((8, held), jnp.float32),
+            dma((2 * CHUNKS + 1,)),
+            dma((CHUNKS + n_col - 1,)),
+            dma((CHUNKS + n_col - 1,)),
+            dma((2 * n_dest,)),
+            dma((2 * n_dest,)),
+            dma((n_col, n_dest)),
+            dma((n_col, n_dest)),
+            dma((n_col, n_dest)),
+            dma((n_col, n_dest)),
+            dma((n_dest,)),
+            dma((n_dest,)),
+        ],
+        compiler_params=pltpu.CompilerParams(
+            collective_id=0, has_side_effects=True, vmem_limit_bytes=40 * 1024 * 1024
+        ),
+        name="dedup_window",
+    )(emb, basis, labels.reshape(1, row_dev), owner_map.reshape(1, nclust), order.reshape(1, row_dev))
+    return best.reshape(row_dev)
+
+
 def solution(mesh):
     return jax.shard_map(
         per_device,

time: 249 us -> 40.6 us (0.16)
  waiting for transfers between devices: 96.3 us -> 0 us
  blocking collectives: 57.3 us -> 0 us
  other arithmetic: 45.6 us -> 0 us
  Pallas kernels: 0 us -> 34.4 us
  between operations: 13.3 us -> 0.01 us
  starting transfers between devices: 10.4 us -> 0 us
  matrix products: 10.3 us -> 0 us
  local copies, waits for them, and re-layouts: 15.2 us -> 6.01 us
    psum x1 -> x0, waiting for transfers between devices: 81.8 us -> none  [per_device(): all_sums, all_counts = lax.psum((sums, counts), ('owners', 'feat', 'rep'))]
    select_n x5 -> x0, other arithmetic: 40.6 us -> none  [the longest x1 39.9 us: per_device(): jnp.take(all_counts, slot)[:, None]]
    psum x1 -> x0, blocking collectives: 35.2 us -> none  [per_device(): all_sums, all_counts = lax.psum((sums, counts), ('owners', 'feat', 'rep'))]
    pallas_call x0 -> x1, Pallas kernels: none -> 34.4 us  [per_device(): pl.pallas_call(functools.partial(window_kernel, n_dest, n_feat, cap), out...]
    all_to_all x1 -> x0, blocking collectives: 18.5 us -> none  [per_device(): lax.all_to_all(vec_buf.reshape(n_dest, cap, width), ('owners', 'feat'), s...]
    all_to_all x3 -> x0, waiting for transfers between devices: 14.4 us -> none  [the longest x1 6.39 us: per_device(): lax.all_to_all(found.reshape(n_dest, cap), ('owners', 'feat'), split_axis...]
    all_to_all x3 -> x0, starting transfers between devices: 10.3 us -> none  [the longest x1 3.64 us: per_device(): lax.all_to_all(order_buf.reshape(n_dest, cap), ('owners', 'feat'), split_...]
    dot_general x3 -> x0, matrix products: 10.3 us -> none  [the longest x1 4.43 us: per_device(): jnp.dot(emb, basis, preferred_element_type=jnp.float32)]
  transfers between devices with their start and end apart: 6 -> 0, of which waited for: 4 -> 0; matrix products, arithmetic and copies ran while one was open for 20% -> 0% of each run, Pallas kernels for 0% -> 0%
where the time goes in v1:
time: 40.6 us; the launch traced here: 40.4 us
  Pallas kernels  34.4 us (85%)
  local copies, waits for them, and re-layouts  6.01 us (15%)
    pallas_call x1, Pallas kernels, per_device(): pl.pallas_call(functools.partial(window_kernel, n_dest, n_feat, cap), out...  34.4 us
    unnamed x11, local copies, waits for them, and re-layouts  6.01 us

profile of v1, /device:TPU:0, one launch (start us, length us, event | category | flops | bytes accessed | tf_op | source)
XLA Modules:
  0.0 40.4 jit_solution(2447557683998277561)
XLA Ops:
  0.0 0.0 copy-start
  0.0 2.2 %copy-done = bf16[1024,2048]{1,0:T(8,128)(2,1)S(1)} copy-done((bf16[1024,2048]{1,0:T(8,128)(2,1)S(1)}, bf16[1024,2048]{1,0:T(8,128)(2,1)}, u32[]{:S(2)}) %copy-start) | copy-done | bytes 4194328
  2.2 0.0 copy-start.1
  2.2 1.2 %copy-done.1 = bf16[2048,256]{1,0:T(8,128)(2,1)S(1)} copy-done((bf16[2048,256]{1,0:T(8,128)(2,1)S(1)}, bf16[2048,256]{1,0:T(8,128)(2,1)}, u32[]{:S(2)}) %copy-start.1) | copy-done | bytes 1048600
  3.4 0.0 copy-start.2
  3.4 0.7 %copy-done.2 = s32[512]{0:T(512)S(1)} copy-done((s32[512]{0:T(512)S(1)}, s32[512]{0:T(512)}, u32[]{:S(2)}) %copy-start.2) | copy-done | bytes 2072
  4.1 0.0 copy-start.3
  4.1 0.7 %copy-done.3 = s32[512]{0:T(512)S(1)} copy-done((s32[512]{0:T(512)S(1)}, s32[512]{0:T(512)}, u32[]{:S(2)}) %copy-start.3) | copy-done | bytes 2072
  4.8 0.0 copy-start.4
  4.8 0.7 %copy-done.4 = s32[64]{0:T(128)S(1)} copy-done((s32[64]{0:T(128)S(1)}, s32[64]{0:T(128)}, u32[]{:S(2)}) %copy-start.4) | copy-done | bytes 280
  5.4 34.4 %dedup_window.1 = f32[1,512]{1,0:T(1,128)S(1)} custom-call(bf16[1024,2048]{1,0:T(8,128)(2,1)S(1)} %copy-done, bf16[2048,256]{1,0:T(8,128)(2,1)S(1)} %copy-done.1, s32[1,512]{1,0:T(1,128)S(1)} %bitcast.5, s32[1,64]{1,0:T(1,128)S(1)} %bitcast.7, s32[1,512]{1,0:T(1,128)S(1)} %bitcast.6), custom_call_target="tpu_custom_call" | custom-call | tf_op jit(solution)/shard_map/dedup_window/pallas_call | solution.py:334
  39.8 0.6 %copy.7 = f32[512]{0:T(512)} copy(f32[512]{0:T(512)S(1)} %bitcast.4) | data formatting | bytes 4096
Async XLA Ops:
  0.0 2.2 %copy-start = (bf16[1024,2048]{1,0:T(8,128)(2,1)S(1)}, bf16[1024,2048]{1,0:T(8,128)(2,1)}, u32[]{:S(2)}) copy-start(bf16[1024,2048]{1,0:T(8,128)(2,1)} %emb.1) | copy-start | bytes 12582916
  2.2 1.2 %copy-start.1 = (bf16[2048,256]{1,0:T(8,128)(2,1)S(1)}, bf16[2048,256]{1,0:T(8,128)(2,1)}, u32[]{:S(2)}) copy-start(bf16[2048,256]{1,0:T(8,128)(2,1)} %basis.1) | copy-start | bytes 3145732
  3.4 0.7 %copy-start.2 = (s32[512]{0:T(512)S(1)}, s32[512]{0:T(512)}, u32[]{:S(2)}) copy-start(s32[512]{0:T(512)} %param.7) | copy-start | bytes 6148
  4.1 0.7 %copy-start.3 = (s32[512]{0:T(512)S(1)}, s32[512]{0:T(512)}, u32[]{:S(2)}) copy-start(s32[512]{0:T(512)} %param.9) | copy-start | bytes 6148
  4.8 0.7 %copy-start.4 = (s32[64]{0:T(128)S(1)}, s32[64]{0:T(128)}, u32[]{:S(2)}) copy-start(s32[64]{0:T(128)} %param.8) | copy-start | bytes 772

commit v2 on v1

--- a/solution.py
+++ b/solution.py
@@ -105,8 +105,8 @@
 
 def window_kernel(
     n_dest, n_feat, cap,
-    emb, basis, labels, owner_map, order, out,
-    emb_v, basis_v, own, part_send, part_recv, place_hot, buf, meta_send, meta, rows, unit,
+    emb, basis, labels_h, owner_map_h, order_h, out,
+    labels, owner_map, order, emb_v, basis_v, own, part_send, part_recv, place_hot, buf, meta_send, meta, rows, unit,
     score_send, back,
     load_sem, part_ssem, part_rsem, meta_ssem, meta_rsem, vec_ssem, vec_rsem,
     fwd_ssem, fwd_rsem, back_ssem, back_rsem,
@@ -147,15 +147,19 @@
         pl.semaphore_signal(barrier, inc=1, device_id=device(column_at(k), other),
                             device_id_type=pl.DeviceIdType.MESH)
 
+    small = [pltpu.make_async_copy(h, v, load_sem.at[2 * CHUNKS + 1 + i]) for i, (h, v) in enumerate(
+        ((labels_h, labels), (owner_map_h, owner_map), (order_h, order)))]
     loads = [pltpu.make_async_copy(basis, basis_v, load_sem.at[2 * CHUNKS])]
     for c in range(2 * CHUNKS):
         side = 1 - feat if c < CHUNKS else feat
         at = pl.multiple_of(side * half + (c % CHUNKS) * step, step)
         loads.append(pltpu.make_async_copy(
             emb.at[pl.ds(at, step), :], emb_v.at[pl.ds(c * step, step), :], load_sem.at[c]))
-    for load in loads:
+    for load in small + loads:
         load.start()
 
+    for load in small:
+        load.wait()
     omap = owner_map[...].astype(f32)
     eye = (lax.broadcasted_iota(jnp.int32, (nclust, nclust), 0)
            == lax.broadcasted_iota(jnp.int32, (nclust, nclust), 1))
@@ -330,13 +334,16 @@
     n_col = width // LANES
     dma = pltpu.SemaphoreType.DMA
     vmem = pl.BlockSpec(memory_space=pltpu.VMEM)
-    hbm = pl.BlockSpec(memory_space=pl.ANY)
+    hbm = pl.BlockSpec(memory_space=pltpu.HBM)
     best = pl.pallas_call(
         functools.partial(window_kernel, n_dest, n_feat, cap),
         out_shape=jax.ShapeDtypeStruct((1, row_dev), jnp.float32),
-        in_specs=[hbm, hbm, vmem, vmem, vmem],
+        in_specs=[hbm] * 5,
         out_specs=vmem,
         scratch_shapes=[
+            pltpu.VMEM((1, row_dev), jnp.int32),
+            pltpu.VMEM((1, nclust), jnp.int32),
+            pltpu.VMEM((1, row_dev), jnp.int32),
             pltpu.VMEM((n_feat * row_dev, depth), jnp.bfloat16),
             pltpu.VMEM((depth, width), jnp.bfloat16),
             pltpu.VMEM((row_dev, width), jnp.float32),
@@ -350,7 +357,7 @@
             pltpu.VMEM((2, held, width), jnp.bfloat16),
             pltpu.VMEM((8, held), jnp.float32),
             pltpu.VMEM((8, held), jnp.float32),
-            dma((2 * CHUNKS + 1,)),
+            dma((2 * CHUNKS + 4,)),
             dma((CHUNKS + n_col - 1,)),
             dma((CHUNKS + n_col - 1,)),
             dma((2 * n_dest,)),
@@ -363,7 +370,7 @@
             dma((n_dest,)),
         ],
         compiler_params=pltpu.CompilerParams(
-            collective_id=0, has_side_effects=True, vmem_limit_bytes=40 * 1024 * 1024
+            collective_id=0, has_side_effects=True, vmem_limit_bytes=60 * 1024 * 1024
         ),
         name="dedup_window",
     )(emb, basis, labels.reshape(1, row_dev), owner_map.reshape(1, nclust), order.reshape(1, row_dev))

time: 40.6 us -> 36.4 us (0.90)
  local copies, waits for them, and re-layouts: 6.01 us -> 1.26 us
  Pallas kernels: 34.4 us -> 35 us
    unnamed x11 -> x1, local copies, waits for them, and re-layouts: 6.01 us -> 1.26 us
    pallas_call x1, Pallas kernels: 34.4 us -> 35 us  [per_device(): pl.pallas_call(functools.partial(window_kernel, n_dest, n_feat, cap), out...]
where the time goes in v2:
time: 36.4 us; the launch traced here: 36.2 us
  Pallas kernels  35 us (96%)
  local copies, waits for them, and re-layouts  1.26 us (3%)
    pallas_call x1, Pallas kernels, per_device(): pl.pallas_call(functools.partial(window_kernel, n_dest, n_feat, cap), out...  35 us
    unnamed x1, local copies, waits for them, and re-layouts  1.26 us

profile of v2, /device:TPU:0, one launch (start us, length us, event | category | flops | bytes accessed | tf_op | source)
XLA Modules:
  0.0 36.2 jit_solution(5577168075801569078)
XLA Ops:
  0.0 35.0 %dedup_window.1 = f32[1,512]{1,0:T(1,128)} custom-call(bf16[1024,2048]{1,0:T(8,128)(2,1)} %emb.1, bf16[2048,256]{1,0:T(8,128)(2,1)} %basis.1, s32[1,512]{1,0:T(1,128)} %bitcast.5, s32[1,64]{1,0:T(1,128)} %bitcast.7, s32[1,512]{1,0:T(1,128)} %bitcast.6), custom_call_target="tpu_custom_call" | custom-call | tf_op jit(solution)/shard_map/dedup_window/pallas_call | solution.py:338
  35.0 1.3 %copy.7 = f32[512]{0:T(512)} copy(f32[512]{0:T(512)} %bitcast.4) | data formatting | bytes 4096

commit v3 on v2

--- a/solution.py
+++ b/solution.py
@@ -108,7 +108,7 @@
     emb, basis, labels_h, owner_map_h, order_h, out,
     labels, owner_map, order, emb_v, basis_v, own, part_send, part_recv, place_hot, buf, meta_send, meta, rows, unit,
     score_send, back,
-    load_sem, part_ssem, part_rsem, meta_ssem, meta_rsem, vec_ssem, vec_rsem,
+    near_sem, load_sem, part_ssem, part_rsem, meta_ssem, meta_rsem, vec_ssem, vec_rsem,
     fwd_ssem, fwd_rsem, back_ssem, back_rsem,
 ):
     f32, bf16 = jnp.float32, jnp.bfloat16
@@ -140,12 +140,27 @@
         )
 
     barrier = pltpu.get_barrier_semaphore()
-    for k in range(n_dest):
-        if k:
-            pl.semaphore_signal(barrier, inc=1, device_id=device(column_at(k), rep),
-                                device_id_type=pl.DeviceIdType.MESH)
-        pl.semaphore_signal(barrier, inc=1, device_id=device(column_at(k), other),
-                            device_id_type=pl.DeviceIdType.MESH)
+    owner = lax.axis_index("owners")
+    n_own = n_dest // n_feat
+    low, high = owner > 0, owner < n_own - 1
+    n_near = 1 + low.astype(jnp.int32) + high.astype(jnp.int32)
+
+    def greet(sem):
+        def signal(to):
+            pl.semaphore_signal(sem, inc=1, device_id=to, device_id_type=pl.DeviceIdType.MESH)
+
+        signal({"feat": 1 - feat})
+
+        @pl.when(low)
+        def _():
+            signal({"owners": owner - 1})
+
+        @pl.when(high)
+        def _():
+            signal({"owners": owner + 1})
+
+    greet(barrier)
+    pl.semaphore_signal(barrier, inc=1, device_id={"rep": other}, device_id_type=pl.DeviceIdType.MESH)
 
     small = [pltpu.make_async_copy(h, v, load_sem.at[2 * CHUNKS + 1 + i]) for i, (h, v) in enumerate(
         ((labels_h, labels), (owner_map_h, owner_map), (order_h, order)))]
@@ -186,7 +201,8 @@
         part_send[at, :] = jnp.dot(
             emb_v[at, :], basis_v[...], preferred_element_type=f32).astype(bf16)
         if c == 0:
-            pl.semaphore_wait(barrier, 2 * n_dest - 1)
+            pl.semaphore_wait(barrier, 1 + n_near)
+            greet(near_sem.at[0])
         cut = (at, pl.ds(0, LANES))
         copy = remote(part_send.at[cut], part_recv.at[cut], part_ssem.at[c], part_rsem.at[c], peer)
         copy.start()
@@ -197,6 +213,13 @@
                       part_rsem.at[CHUNKS + n - 1], peer)
         copy.start()
         part_copies[n].append(copy)
+
+    def hear(c):
+        pl.semaphore_wait(near_sem.at[c], n_near)
+        if c < n_own - 2:
+            greet(near_sem.at[c + 1])
+
+    hear(0)
 
     place_hot[...] = jnp.where(
         lax.broadcasted_iota(jnp.int32, (held, half), 0) == place, 1.0, 0.0).astype(bf16)
@@ -212,25 +235,25 @@
     meta_send[...] = jnp.zeros_like(meta_send)
     meta_send[0:1, :] = placed[0:1, :]
     meta_send[1:2, :] = placed[1:2, :] * 16384.0 + placed[2:3, :] * 128.0 + placed[3:4, :]
-    meta_copies = []
-    for k in range(n_dest):
-        to = column_at(k)
-        if k:
-            meta_copies.append(remote(
-                meta_send.at[:, block(to)], meta.at[0, :, block(me)],
-                meta_ssem.at[k], meta_rsem.at[k], device(to, rep)))
-        meta_copies.append(remote(
-            meta_send.at[:, block(to)], meta.at[1, :, block(me)],
-            meta_ssem.at[n_dest + k], meta_rsem.at[n_dest + k], device(to, other)))
-    for copy in meta_copies:
-        copy.start()
-    meta[0, :, block(me)] = meta_send[:, block(me)]
+    hear(1)
 
     for c in range(CHUNKS):
         at = pl.ds(c * step, step)
         loads[1 + CHUNKS + c].wait()
         own[at, :] = jnp.dot(
             emb_v[pl.ds((CHUNKS + c) * step, step), :], basis_v[...], preferred_element_type=f32)
+
+    hear(2)
+    meta_copies = [None]
+    for k in range(1, n_dest):
+        to = column_at(k)
+        copy = remote(meta_send.at[:, block(to)], meta.at[0, :, block(me)],
+                      meta_ssem.at[k], meta_rsem.at[k], device(to, rep))
+        copy.start()
+        meta_copies.append(copy)
+    meta[0, :, block(me)] = meta_send[:, block(me)]
+
+    order_of_sends = sorted(range(1, n_dest), key=lambda k: -min(k, n_dest - k))
 
     vec_copies = [[None] * n_dest for _ in range(n_col)]
     for n in range(n_col):
@@ -239,7 +262,7 @@
             copy.wait_recv()
         proj = (own[:, lanes] + part_recv[:, lanes].astype(f32)).astype(bf16)
         buf[:, lanes] = jnp.dot(place_hot[...], proj, preferred_element_type=f32).astype(bf16)
-        for k in range(1, n_dest):
+        for k in order_of_sends:
             to = column_at(k)
             copy = remote(buf.at[block(to), lanes], rows.at[0, block(me), lanes],
                           vec_ssem.at[n, k], vec_rsem.at[n, k], device(to, rep))
@@ -250,8 +273,11 @@
         for copy in copies:
             copy.wait_send()
 
-    for copy in meta_copies:
+    for copy in meta_copies[1:]:
         copy.wait()
+    copy = remote(meta.at[0], meta.at[1], meta_ssem.at[0], meta_rsem.at[0], {"rep": other})
+    copy.start()
+    copy.wait()
     member = lax.broadcasted_iota(jnp.int32, (8, held), 0).astype(f32) + 1.0
     hot = [jnp.where(meta[r, 0:1, :] == member, 1.0, 0.0) for r in range(2)]
     counts = jnp.sum(hot[0], axis=1, keepdims=True) + jnp.sum(hot[1], axis=1, keepdims=True)
@@ -326,7 +352,7 @@
     nclust = owner_map.shape[0]
     fits = (
         n_feat == 2 and lax.axis_size("rep") == 2 and cap % LANES == 0 and width == 2 * LANES
-        and row_dev % (16 * CHUNKS) == 0 and nclust == 8 * n_dest and n_dest <= 8
+        and row_dev % (16 * CHUNKS) == 0 and nclust == 8 * n_dest and lax.axis_size("owners") == 4
     )
     if not fits:
         return per_device_plain(emb, basis, labels, owner_map, order)
@@ -357,11 +383,12 @@
             pltpu.VMEM((2, held, width), jnp.bfloat16),
             pltpu.VMEM((8, held), jnp.float32),
             pltpu.VMEM((8, held), jnp.float32),
+            pltpu.SemaphoreType.REGULAR((CHUNKS,)),
             dma((2 * CHUNKS + 4,)),
             dma((CHUNKS + n_col - 1,)),
             dma((CHUNKS + n_col - 1,)),
-            dma((2 * n_dest,)),
-            dma((2 * n_dest,)),
+            dma((n_dest,)),
+            dma((n_dest,)),
             dma((n_col, n_dest)),
             dma((n_col, n_dest)),
             dma((n_col, n_dest)),

time: 36.4 us -> 34.3 us (0.942)
  Pallas kernels: 35 us -> 32.8 us
    pallas_call x1, Pallas kernels: 35 us -> 32.8 us  [per_device(): pl.pallas_call(functools.partial(window_kernel, n_dest, n_feat, cap), out...]
where the time goes in v3:
time: 34.3 us; the launch traced here: 34.1 us
  Pallas kernels  32.8 us (96%)
  local copies, waits for them, and re-layouts  1.26 us (4%)
    pallas_call x1, Pallas kernels, per_device(): pl.pallas_call(functools.partial(window_kernel, n_dest, n_feat, cap), out...  32.8 us
    unnamed x1, local copies, waits for them, and re-layouts  1.26 us

profile of v3, /device:TPU:0, one launch (start us, length us, event | category | flops | bytes accessed | tf_op | source)
XLA Modules:
  0.0 34.1 jit_solution(16080916676712409260)
XLA Ops:
  0.0 32.8 %dedup_window.1 = f32[1,512]{1,0:T(1,128)} custom-call(bf16[1024,2048]{1,0:T(8,128)(2,1)} %emb.1, bf16[2048,256]{1,0:T(8,128)(2,1)} %basis.1, s32[1,512]{1,0:T(1,128)} %bitcast.5, s32[1,64]{1,0:T(1,128)} %bitcast.7, s32[1,512]{1,0:T(1,128)} %bitcast.6), custom_call_target="tpu_custom_call" | custom-call | tf_op jit(solution)/shard_map/dedup_window/pallas_call | solution.py:364
  32.8 1.3 %copy.7 = f32[512]{0:T(512)} copy(f32[512]{0:T(512)} %bitcast.4) | data formatting | bytes 4096

commit v4 on v3

--- a/solution.py
+++ b/solution.py
@@ -173,25 +173,6 @@
     for load in small + loads:
         load.start()
 
-    for load in small:
-        load.wait()
-    omap = owner_map[...].astype(f32)
-    eye = (lax.broadcasted_iota(jnp.int32, (nclust, nclust), 0)
-           == lax.broadcasted_iota(jnp.int32, (nclust, nclust), 1))
-    omap_col = jnp.sum(jnp.where(eye, omap, 0.0), axis=1, keepdims=True)
-    label_hot = lax.broadcasted_iota(jnp.int32, (nclust, half), 0) == labels[...]
-    slot = jnp.sum(jnp.where(label_hot, omap_col, 0.0), axis=0, keepdims=True)
-    dest = jnp.floor(slot * (1.0 / cl_dest))
-    local = slot - dest * cl_dest
-    dest_hot = lax.broadcasted_iota(jnp.int32, (n_dest, half), 0) == dest.astype(jnp.int32)
-    upto = (lax.broadcasted_iota(jnp.int32, (half, half), 0)
-            <= lax.broadcasted_iota(jnp.int32, (half, half), 1))
-    running = jnp.dot(
-        jnp.where(dest_hot, 1.0, 0.0).astype(bf16), jnp.where(upto, 1.0, 0.0).astype(bf16),
-        preferred_element_type=f32)
-    rank = jnp.sum(jnp.where(dest_hot, running, 0.0), axis=0, keepdims=True) - 1.0
-    place = (dest * cap + rank).astype(jnp.int32)
-
     peer = {"feat": 1 - feat}
     part_copies = [[], []]
     loads[0].wait()
@@ -219,6 +200,25 @@
         if c < n_own - 2:
             greet(near_sem.at[c + 1])
 
+    for load in small:
+        load.wait()
+    omap = owner_map[...].astype(f32)
+    eye = (lax.broadcasted_iota(jnp.int32, (nclust, nclust), 0)
+           == lax.broadcasted_iota(jnp.int32, (nclust, nclust), 1))
+    omap_col = jnp.sum(jnp.where(eye, omap, 0.0), axis=1, keepdims=True)
+    label_hot = lax.broadcasted_iota(jnp.int32, (nclust, half), 0) == labels[...]
+    slot = jnp.sum(jnp.where(label_hot, omap_col, 0.0), axis=0, keepdims=True)
+    dest = jnp.floor(slot * (1.0 / cl_dest))
+    local = slot - dest * cl_dest
+    dest_hot = lax.broadcasted_iota(jnp.int32, (n_dest, half), 0) == dest.astype(jnp.int32)
+    upto = (lax.broadcasted_iota(jnp.int32, (half, half), 0)
+            <= lax.broadcasted_iota(jnp.int32, (half, half), 1))
+    running = jnp.dot(
+        jnp.where(dest_hot, 1.0, 0.0).astype(bf16), jnp.where(upto, 1.0, 0.0).astype(bf16),
+        preferred_element_type=f32)
+    rank = jnp.sum(jnp.where(dest_hot, running, 0.0), axis=0, keepdims=True) - 1.0
+    place = (dest * cap + rank).astype(jnp.int32)
+
     hear(0)
 
     place_hot[...] = jnp.where(
@@ -253,21 +253,31 @@
         meta_copies.append(copy)
     meta[0, :, block(me)] = meta_send[:, block(me)]
 
-    order_of_sends = sorted(range(1, n_dest), key=lambda k: -min(k, n_dest - k))
-
+    side = owner // (n_own // 2)
+    ways = [(o, x) for o in (3 * (1 - side), 2 - side, 4 * side + 1 - owner, owner) for x in (feat, 1 - feat)]
+    ways = ways[:-2] + [ways[-1]]
     vec_copies = [[None] * n_dest for _ in range(n_col)]
     for n in range(n_col):
         lanes = pl.ds(n * LANES, LANES)
         for copy in part_copies[n]:
             copy.wait_recv()
         proj = (own[:, lanes] + part_recv[:, lanes].astype(f32)).astype(bf16)
-        buf[:, lanes] = jnp.dot(place_hot[...], proj, preferred_element_type=f32).astype(bf16)
-        for k in order_of_sends:
-            to = column_at(k)
-            copy = remote(buf.at[block(to), lanes], rows.at[0, block(me), lanes],
+
+        def put(column):
+            buf[block(column), lanes] = jnp.dot(
+                place_hot[block(column), :], proj, preferred_element_type=f32).astype(bf16)
+
+        def send(to, k):
+            return remote(buf.at[block(to), lanes], rows.at[0, block(me), lanes],
                           vec_ssem.at[n, k], vec_rsem.at[n, k], device(to, rep))
-            copy.start()
-            vec_copies[n][k] = copy
+
+        for o, x in ways:
+            to = o * n_feat + x
+            put(to)
+            send(to, lax.rem(to - me + n_dest, n_dest)).start()
+        for k in range(1, n_dest):
+            vec_copies[n][k] = send(column_at(k), k)
+        put(me)
         rows[0, block(me), lanes] = buf[block(me), lanes]
     for copies in part_copies:
         for copy in copies:

time: 34.3 us -> 33.6 us (0.980)
  Pallas kernels: 32.8 us -> 32.2 us
    pallas_call x1, Pallas kernels: 32.8 us -> 32.2 us  [per_device(): pl.pallas_call(functools.partial(window_kernel, n_dest, n_feat, cap), out...]
where the time goes in v4:
time: 33.6 us; the launch traced here: 33.4 us
  Pallas kernels  32.2 us (96%)
  local copies, waits for them, and re-layouts  1.26 us (4%)
    pallas_call x1, Pallas kernels, per_device(): pl.pallas_call(functools.partial(window_kernel, n_dest, n_feat, cap), out...  32.2 us
    unnamed x1, local copies, waits for them, and re-layouts  1.26 us

profile of v4, /device:TPU:0, one launch (start us, length us, event | category | flops | bytes accessed | tf_op | source)
XLA Modules:
  0.0 33.4 jit_solution(17098057209903185842)
XLA Ops:
  0.0 32.2 %dedup_window.1 = f32[1,512]{1,0:T(1,128)} custom-call(bf16[1024,2048]{1,0:T(8,128)(2,1)} %emb.1, bf16[2048,256]{1,0:T(8,128)(2,1)} %basis.1, s32[1,512]{1,0:T(1,128)} %bitcast.5, s32[1,64]{1,0:T(1,128)} %bitcast.7, s32[1,512]{1,0:T(1,128)} %bitcast.6), custom_call_target="tpu_custom_call" | custom-call | tf_op jit(solution)/shard_map/dedup_window/pallas_call | solution.py:374
  32.2 1.3 %copy.7 = f32[512]{0:T(512)} copy(f32[512]{0:T(512)} %bitcast.4) | data formatting | bytes 4096
